TPU v7x, 256 devices: a whole 4x4x8 slice. The times are simulated.
256 devices in a mesh: scen: 16 (over z_lo, x), row: 2 (over core), col: 8 (over y, z_hi).
Axes of the slice: x: 4, y: 4, z: 8 (z_hi: 2, z_lo: 4; z = z_hi * 4 + z_lo), core: 2. Of those that a mesh axis runs over, the one named last changes fastest.
Arguments:
- kkt: float32 [48, 768, 768], P('scen', ('row', 'col')), as said below
- border: float32 [48, 768, 4096], P('scen', None, ('row', 'col')), may hold values from -0.15625 to 0.15625
- first_diag: float32 [4096], P('scen'), may hold values from 0.5 to 1.5
- assignment: int32 [48], P('scen'), may hold values from 0 to 47, as said below
- panel: int32 [8], replicated, may hold values from 0 to 7, each once
Outputs:
- schur: float32 [4096, 4096], P('scen', ('row', 'col'))
- panel_factor: float32 [4096, 512], P('scen', ('row', 'col'))
Inputs may be any that keep to these rules, and one draw needn't show every extreme that they name: assignment is a permutation; with k = d * 3 + j (0 <= j < 3), assignment[k] is either k or (d XOR 1) * 3 + j, and the two scenarios of such a pair are either both fixed or swapped. panel is a permutation. Each kkt block is symmetric positive definite; after scaling by its diagonal, the off-diagonal part has spectral norm about one half.
All inputs are finite; a program needn't handle non-finite values.
Results may differ from a plain program's by a relative error of at most 0.00015.
Values sent between devices are 32-bit elements; how exact they have to be, the bound alone decides.
No kernel may reach another device: no remote copies, remote signals or barrier semaphores. Data moves between devices by JAX's collectives and lax.ppermute only.
A program may use at most 128 MiB of HBM per device.

v0:
```python
import jax
import jax.numpy as jnp
from jax import lax
from jax.sharding import PartitionSpec as P

NK = 768
NF = 4096
PW = 512
NEWTON = 3


HIGH = lax.Precision.HIGHEST


def swapped(value, axis, distance):
    mask = 2**distance
    pairs = [(source, source ^ mask) for source in range(lax.axis_size(axis))]
    return lax.ppermute(value, axis, pairs)


def matmul(left, right):
    return jnp.dot(left, right, precision=HIGH, preferred_element_type=jnp.float32)


def contract(left, right):
    return lax.dot_general(
        left, right, (((0,), (0,)), ((), ())), precision=HIGH, preferred_element_type=jnp.float32
    )


def body(kkt, border, first_diag, assignment, panel):
    scen_index = lax.axis_index("scen")
    own_index = lax.axis_index(("row", "col"))
    slots = kkt.shape[0]
    partner = swapped(border, "scen", 0)
    kkt_all = lax.all_gather(kkt, ("row", "col"), axis=1, tiled=True)
    row_count = kkt.shape[1]
    col_count = border.shape[2]
    first_row = own_index * row_count
    row_ids = first_row + jnp.arange(row_count, dtype=jnp.int32)
    eye_rows = (jnp.arange(NK, dtype=jnp.int32)[None, :] == row_ids[:, None]).astype(jnp.float32)
    tile_total = jnp.zeros((NF, col_count), jnp.float32)
    for slot in range(slots):
        scenario_id = scen_index * slots + slot
        chosen = jnp.where(assignment[slot] == scenario_id, border[slot], partner[slot])
        kkt_rows = kkt[slot]
        kkt_full = kkt_all[slot]
        inv_diag = 1.0 / jnp.diagonal(kkt_full)
        local_inv = lax.dynamic_slice_in_dim(inv_diag, first_row, row_count)
        approx = (
            2.0 * (eye_rows * local_inv[:, None])
            - local_inv[:, None] * kkt_rows * inv_diag[None, :]
        )
        for step in range(NEWTON - 1):
            left = matmul(approx, kkt_full)

            def add_block(total, piece, start, left=left):
                return matmul(left, piece)

            product = add_block(
                jnp.zeros_like(approx),
                lax.all_gather(approx, ("row", "col"), axis=0, tiled=True),
                jnp.int32(0),
            )
            approx = 2.0 * approx - product

        def solve_piece(piece, start, chosen=chosen):
            return matmul(piece, chosen)

        solved = solve_piece(
            lax.all_gather(approx, ("row", "col"), axis=0, tiled=True), jnp.int32(0)
        )

        def solved_piece(piece, start, chosen=chosen):
            return contract(piece, chosen)

        tile = solved_piece(
            lax.all_gather(solved, ("row", "col"), axis=1, tiled=True), jnp.int32(0)
        )
        tile_total = tile_total + tile
    summed = lax.psum_scatter(tile_total, "scen", scatter_dimension=0, tiled=True)
    row_span = summed.shape[0]
    global_rows = scen_index * row_span + jnp.arange(row_span, dtype=jnp.int32)
    global_cols = own_index * col_count + jnp.arange(col_count, dtype=jnp.int32)
    on_diag = global_rows[:, None] == global_cols[None, :]
    schur = summed + jnp.where(on_diag, first_diag[:, None], 0.0)
    panel_start = panel[0] * PW
    panel_ids = panel_start + jnp.arange(PW, dtype=jnp.int32)
    select_cols = (global_cols[:, None] == panel_ids[None, :]).astype(jnp.float32)
    select_rows = (panel_ids[:, None] == global_rows[None, :]).astype(jnp.float32)
    panel_rows = lax.psum(matmul(schur, select_cols), ("row", "col"))
    block = lax.psum(matmul(select_rows, panel_rows), "scen")
    symmetric = 0.5 * (block + block.T)
    lower_factor = jnp.linalg.cholesky(symmetric)
    factor = lax.linalg.triangular_solve(
        lower_factor, panel_rows, left_side=False, lower=True, transpose_a=True
    )
    share = PW // lax.axis_size(("row", "col"))
    own_cols = lax.dynamic_slice_in_dim(factor, own_index * share, share, 1)
    return (schur, own_cols)


def solution(mesh):
    in_specs = (
        P("scen", ("row", "col"), None),
        P("scen", None, ("row", "col")),
        P("scen"),
        P("scen"),
        P(),
    )
    out_specs = (P("scen", ("row", "col")), P("scen", ("row", "col")))
    return jax.shard_map(body, mesh=mesh, in_specs=in_specs, out_specs=out_specs, check_vma=False)
```

profile of v0, /device:TPU:32, one launch (start us, length us, event | category | flops | bytes accessed | tf_op | source)
XLA Modules:
  0.0 1767.7 jit_solution(16191081904364265185)
XLA Ops:
  8.0 103.2 %all-gather.14.cloned.1.call-done = f32[3,768,768]{2,1,0:T(8,128)} async-done(((f32[3,48,768]{2,1,0:T(8,128)}), f32[3,768,768]{2,1,0:T(8,128)}) %all-gather.14.cloned.1.call-update) | async-done | bytes 7077904 | tf_op jit(solution)/shard_map/all_gather | solution.py:36
  111.2 5.7 slice_bitcast_fusion.2
  116.9 12.8 gather_fusion.2
  129.7 12.0 gather_fusion.1
  141.7 6.3 gather_fusion
  150.5 3.2 fusion.38
  153.7 54.7 %all-gather.32.cloned.1.call-done = f32[768,768]{1,0:T(8,128)} async-done(((f32[48,768]{1,0:T(8,128)}), f32[768,768]{1,0:T(8,128)}) %all-gather.32.cloned.1.call-update) | async-done | bytes 2359312 | tf_op jit(solution)/shard_map/all_gather | solution.py:62
  208.4 3.8 convolution_subtract_fusion.2
  212.3 3.2 fusion.42
  215.5 56.3 %all-gather.24.cloned.1.call-done = f32[768,768]{1,0:T(8,128)} async-done(((f32[48,768]{1,0:T(8,128)}), f32[768,768]{1,0:T(8,128)}) %all-gather.24.cloned.1.call-update) | async-done | bytes 2359312 | tf_op jit(solution)/shard_map/all_gather | solution.py:62
  271.8 3.8 convolution_subtract_fusion.4
  275.7 3.2 fusion.46
  279.0 56.7 %all-gather.16.cloned.1.call-done = f32[768,768]{1,0:T(8,128)} async-done(((f32[48,768]{1,0:T(8,128)}), f32[768,768]{1,0:T(8,128)}) %all-gather.16.cloned.1.call-update) | async-done | bytes 2359312 | tf_op jit(solution)/shard_map/all_gather | solution.py:62
  335.7 3.8 convolution_subtract_fusion.6
  339.7 3.2 fusion.110
  342.9 56.0 %all-gather.34.cloned.1.call-done = f32[768,768]{1,0:T(8,128)} async-done(((f32[48,768]{1,0:T(8,128)}), f32[768,768]{1,0:T(8,128)}) %all-gather.34.cloned.1.call-update) | async-done | bytes 2359312 | tf_op jit(solution)/shard_map/all_gather | solution.py:62
  398.9 3.8 convolution_subtract_fusion.1
  402.8 3.2 fusion.109
  406.0 56.2 %all-gather.26.cloned.1.call-done = f32[768,768]{1,0:T(8,128)} async-done(((f32[48,768]{1,0:T(8,128)}), f32[768,768]{1,0:T(8,128)}) %all-gather.26.cloned.1.call-update) | async-done | bytes 2359312 | tf_op jit(solution)/shard_map/all_gather | solution.py:62
  462.2 3.8 convolution_subtract_fusion.3
  466.1 3.3 fusion.108
  469.4 56.2 %all-gather.18.cloned.1.call-done = f32[768,768]{1,0:T(8,128)} async-done(((f32[48,768]{1,0:T(8,128)}), f32[768,768]{1,0:T(8,128)}) %all-gather.18.cloned.1.call-update) | async-done | bytes 2359312 | tf_op jit(solution)/shard_map/all_gather | solution.py:62
  525.6 3.8 convolution_subtract_fusion.5
  532.3 50.8 %collective-permute-done = f32[3,768,256]{2,1,0:T(8,128)} collective-permute-done((f32[3,768,256]{2,1,0:T(8,128)S(1)}, f32[3,768,256]{2,1,0:T(8,128)}, u32[]{:S(2)}, u32[]{:S(2)}) %collective-permute-start) | collective-permute-done | bytes 2359328 | tf_op jit(solution)/shard_map/ppermute | solution.py:18
  583.1 6.5 all-gather.36.cloned.1.call-done
  589.6 4.7 fusion.32
  595.1 57.9 %all-gather.28.cloned.1.call-done = f32[768,768]{1,0:T(8,128)} async-done(((f32[48,768]{1,0:T(8,128)}), f32[768,768]{1,0:T(8,128)}) %all-gather.28.cloned.1.call-update) | async-done | bytes 2359312 | tf_op jit(solution)/shard_map/all_gather | solution.py:71
  653.0 4.7 fusion.28
  658.4 57.8 %all-gather.20.cloned.1.call-done = f32[768,768]{1,0:T(8,128)} async-done(((f32[48,768]{1,0:T(8,128)}), f32[768,768]{1,0:T(8,128)}) %all-gather.20.cloned.1.call-update) | async-done | bytes 2359312 | tf_op jit(solution)/shard_map/all_gather | solution.py:71
  716.2 4.8 fusion.24
  721.1 143.3 %all-gather.38.cloned.1.call-done = f32[768,4096]{1,0:T(8,128)} async-done(((f32[768,256]{1,0:T(8,128)}), f32[768,4096]{1,0:T(8,128)}) %all-gather.38.cloned.1.call-update) | async-done | bytes 12582928 | tf_op jit(solution)/shard_map/all_gather | solution.py:78
  864.4 24.2 %fusion.30 = f32[4096,256]{1,0:T(8,128)} fusion(f32[768,4096]{1,0:T(8,128)} %all-gather.38.cloned.1.call-done, f32[3,768,256]{2,1,0:T(8,128)} %collective-permute-done, f32[3,768,256]{2,1,0:T(8,128)S(1)} %copy-done, pred[]{:T(512)S(6)} %eq.90), kind=kOutput, calls=%fused_computation.61 | convolution fusion | flops 9663873024 | bytes 18350080 | tf_op jit(solution)/shard_map/dot_general | solution.py:26
  888.6 122.7 %all-gather.30.cloned.1.call-done = f32[768,4096]{1,0:T(8,128)} async-done(((f32[768,256]{1,0:T(8,128)}), f32[768,4096]{1,0:T(8,128)}) %all-gather.30.cloned.1.call-update) | async-done | bytes 12582928 | tf_op jit(solution)/shard_map/all_gather | solution.py:78
  1011.3 24.7 %fusion.26 = f32[4096,256]{1,0:T(8,128)} fusion(f32[768,4096]{1,0:T(8,128)} %all-gather.30.cloned.1.call-done, f32[3,768,256]{2,1,0:T(8,128)} %collective-permute-done, f32[3,768,256]{2,1,0:T(8,128)S(1)} %copy-done, pred[]{:T(512)S(6)} %eq.89), kind=kOutput, calls=%fused_computation.59 | convolution fusion | flops 9663873024 | bytes 18350080 | tf_op jit(solution)/shard_map/dot_general | solution.py:26
  1036.0 122.3 %all-gather.22.cloned.1.call-done = f32[768,4096]{1,0:T(8,128)} async-done(((f32[768,256]{1,0:T(8,128)}), f32[768,4096]{1,0:T(8,128)}) %all-gather.22.cloned.1.call-update) | async-done | bytes 12582928 | tf_op jit(solution)/shard_map/all_gather | solution.py:78
  1158.4 26.2 %fusion = f32[4096,256]{1,0:T(8,128)} fusion(f32[4096,256]{1,0:T(8,128)} %fusion.30, f32[4096,256]{1,0:T(8,128)} %fusion.26, f32[768,4096]{1,0:T(8,128)} %all-gather.22.cloned.1.call-done, f32[3,768,256]{2,1,0:T(8,128)} %collective-permute-done, f32[3,768,256]{2,1,0:T(8,128)S(1)} %copy-done, pred[]{:T(512)S(6)} %eq.88), kind=kOutput, calls=%fused_computation.6 | convolution fusion | flops 9665970176 | bytes 26738688 | tf_op jit(solution)/shard_map/dot_general | solution.py:26
  1185.3 82.1 %reduce-scatter.2.cloned.1.call-done = f32[256,256]{1,0:T(8,128)} async-done(((f32[4096,256]{1,0:T(8,128)}), f32[256,256]{1,0:T(8,128)}) %reduce-scatter.2.cloned.1.call-update) | async-done | bytes 262160 | tf_op jit(solution)/shard_map/reduce_scatter | solution.py:81
  1270.1 189.3 %all-reduce.4.cloned.1.call-done = f32[256,512]{1,0:T(8,128)} async-done(((f32[256,512]{1,0:T(8,128)}), f32[256,512]{1,0:T(8,128)}) %all-reduce.4.cloned.1.call-update) | async-done | bytes 524304 | tf_op jit(solution)/shard_map/psum | solution.py:91
  1462.2 154.5 %all-reduce.6.cloned.1.call-done = f32[512,512]{0,1:T(8,128)} async-done(((f32[512,512]{0,1:T(8,128)}), f32[512,512]{0,1:T(8,128)}) %all-reduce.6.cloned.1.call-update) | async-done | bytes 1048592 | tf_op jit(solution)/shard_map/psum | solution.py:92
  1619.2 11.7 cholesky.104
  1631.1 9.8 custom-call.30
  1641.5 12.1 cholesky.217
  1653.7 9.8 custom-call.31
  1664.2 11.7 cholesky.238
  1675.9 9.8 custom-call.32
  1686.3 11.9 cholesky.255
  1703.5 10.0 while.1
  1713.5 40.1 %custom-call.33 = f32[4,128,128]{1,2,0:T(8,128)S(1)} custom-call(f32[4,128,128]{2,1,0:T(8,128)} %get-tuple-element.9), custom_call_target="InvertDiagBlocksLowerTriangular" | custom-call | tf_op jit(solution)/shard_map/triangular_solve | solution.py:95
  (119 shorter events, 37.1 us)
Async XLA Ops:
  7.2 104.0 %all-gather.14.cloned.1.call-start = ((), (), s32[]{:S(2)}) async-start(), calls=%async_computation.1 | async-start | bytes 7520256 | tf_op jit(solution)/shard_map/all_gather | solution.py:36
  7.9 200.5 %all-gather.32.cloned.1.call-start = ((), (), s32[]{:S(2)}) async-start(), calls=%async_computation.10 | async-start | bytes 2506752 | tf_op jit(solution)/shard_map/all_gather | solution.py:62
  141.7 6.6 copy-start.2
  149.1 59.3 %copy-start.8 = (f32[48,768]{1,0:T(8,128)S(1)}, f32[48,768]{1,0:T(8,128)}, u32[]{:S(2)}) copy-start(f32[48,768]{1,0:T(8,128)} %get-tuple-element.24) | copy-start | bytes 442372
  149.2 122.7 %all-gather.24.cloned.1.call-start = ((), (), s32[]{:S(2)}) async-start(), calls=%async_computation.6 | async-start | bytes 2506752 | tf_op jit(solution)/shard_map/all_gather | solution.py:62
  149.9 185.8 %all-gather.16.cloned.1.call-start = ((), (), s32[]{:S(2)}) async-start(), calls=%async_computation.2 | async-start | bytes 2506752 | tf_op jit(solution)/shard_map/all_gather | solution.py:62
  150.5 248.4 %all-gather.34.cloned.1.call-start = ((), (), s32[]{:S(2)}) async-start(), calls=%async_computation.11 | async-start | bytes 2506752 | tf_op jit(solution)/shard_map/all_gather | solution.py:62
  153.7 118.1 %copy-start.7 = (f32[48,768]{1,0:T(8,128)S(1)}, f32[48,768]{1,0:T(8,128)}, u32[]{:S(2)}) copy-start(f32[48,768]{1,0:T(8,128)} %get-tuple-element.25) | copy-start | bytes 442372
  212.3 249.9 %all-gather.26.cloned.1.call-start = ((), (), s32[]{:S(2)}) async-start(), calls=%async_computation.7 | async-start | bytes 2506752 | tf_op jit(solution)/shard_map/all_gather | solution.py:62
  215.5 120.1 %copy-start.6 = (f32[48,768]{1,0:T(8,128)S(1)}, f32[48,768]{1,0:T(8,128)}, u32[]{:S(2)}) copy-start(f32[48,768]{1,0:T(8,128)} %get-tuple-element.23) | copy-start | bytes 442372
  275.7 64.1 %copy-start.3 = (f32[48,768]{1,0:T(8,128)S(1)}, f32[48,768]{1,0:T(8,128)}, u32[]{:S(2)}) copy-start(f32[48,768]{1,0:T(8,128)} %convolution_subtract_fusion.2) | copy-start | bytes 442372
  275.7 249.9 %all-gather.18.cloned.1.call-start = ((), (), s32[]{:S(2)}) async-start(), calls=%async_computation.3 | async-start | bytes 2506752 | tf_op jit(solution)/shard_map/all_gather | solution.py:62
  339.5 63.3 %copy-start.4 = (f32[48,768]{1,0:T(8,128)S(1)}, f32[48,768]{1,0:T(8,128)}, u32[]{:S(2)}) copy-start(f32[48,768]{1,0:T(8,128)} %convolution_subtract_fusion.4) | copy-start | bytes 442372
  339.5 250.1 %all-gather.36.cloned.1.call-start = ((), (), s32[]{:S(2)}) async-start(), calls=%async_computation.12 | async-start | bytes 2506752 | tf_op jit(solution)/shard_map/all_gather | solution.py:71
  402.8 63.3 %copy-start.5 = (f32[48,768]{1,0:T(8,128)S(1)}, f32[48,768]{1,0:T(8,128)}, u32[]{:S(2)}) copy-start(f32[48,768]{1,0:T(8,128)} %convolution_subtract_fusion.6) | copy-start | bytes 442372
  402.8 250.2 %all-gather.28.cloned.1.call-start = ((), (), s32[]{:S(2)}) async-start(), calls=%async_computation.8 | async-start | bytes 2506752 | tf_op jit(solution)/shard_map/all_gather | solution.py:71
  466.0 63.5 %copy-start = (f32[3,768,256]{2,1,0:T(8,128)S(1)}, f32[3,768,256]{2,1,0:T(8,128)}, u32[]{:S(2)}) copy-start(f32[3,768,256]{2,1,0:T(8,128)} %param.6) | copy-start | bytes 7077892
  466.0 65.0 %copy-start.10 = (s32[3]{0:T(128)S(1)}, s32[3]{0:T(128)}, u32[]{:S(2)}) copy-start(s32[3]{0:T(128)} %param.8) | copy-start | bytes 40
  466.0 250.2 %all-gather.20.cloned.1.call-start = ((), (), s32[]{:S(2)}) async-start(), calls=%async_computation.4 | async-start | bytes 2506752 | tf_op jit(solution)/shard_map/all_gather | solution.py:71
  529.4 334.9 %all-gather.38.cloned.1.call-start = ((), (), s32[]{:S(2)}) async-start(), calls=%async_computation.13 | async-start | bytes 13369344 | tf_op jit(solution)/shard_map/all_gather | solution.py:78
  529.5 53.6 %collective-permute-start = (f32[3,768,256]{2,1,0:T(8,128)S(1)}, f32[3,768,256]{2,1,0:T(8,128)}, u32[]{:S(2)}, u32[]{:S(2)}) collective-permute-start(f32[3,768,256]{2,1,0:T(8,128)S(1)} %copy-done), channel_id=1, source_target_pairs={{0,16},{16,0},{32,48},{48,32},{64,80},{80,64},{96,112},{112,96},{1... | collective-permute-start | bytes 7077896 | tf_op jit(solution)/shard_map/ppermute | solution.py:18
  594.3 417.0 %all-gather.30.cloned.1.call-start = ((), (), s32[]{:S(2)}) async-start(), calls=%async_computation.9 | async-start | bytes 13369344 | tf_op jit(solution)/shard_map/all_gather | solution.py:78
  657.7 500.6 %all-gather.22.cloned.1.call-start = ((), (), s32[]{:S(2)}) async-start(), calls=%async_computation.5 | async-start | bytes 13369344 | tf_op jit(solution)/shard_map/all_gather | solution.py:78
  721.0 546.4 %reduce-scatter.2.cloned.1.call-start = ((), (), s32[]{:S(2)}) async-start(), calls=%async_computation.14 | async-start | bytes 4456448 | tf_op jit(solution)/shard_map/reduce_scatter | solution.py:81
  1184.6 0.7 copy-start.12
  1184.6 82.9 %copy-start.11 = (f32[256]{0:T(256)S(1)}, f32[256]{0:T(256)}, u32[]{:S(2)}) copy-start(f32[256]{0:T(256)} %param.7) | copy-start | bytes 3076
  1184.6 274.8 %all-reduce.4.cloned.1.call-start = ((), (), s32[]{:S(2)}) async-start(), calls=%async_computation.15 | async-start | bytes 1048576 | tf_op jit(solution)/shard_map/psum | solution.py:91
  1268.5 349.8 %copy-start.9 = (f32[256,256]{1,0:T(8,128)}, f32[256,256]{1,0:T(8,128)S(1)}, u32[]{:S(2)}) copy-start(f32[256,256]{1,0:T(8,128)S(1)} %select_add_fusion) | copy-start | bytes 786436
  1269.9 346.8 %all-reduce.6.cloned.1.call-start = ((), (), s32[]{:S(2)}) async-start(), calls=%async_computation.16 | async-start | bytes 2097152 | tf_op jit(solution)/shard_map/psum | solution.py:92
  1616.7 1.7 copy-start.1
Sparse Core Ops, SparseCore 0:
  10.9 100.3 all-gather.13
  149.3 59.0 all-gather.31
  211.1 60.6 all-gather.23
  275.0 60.6 all-gather.15
  338.2 60.6 all-gather.33
  401.5 60.6 all-gather.25
  464.9 60.6 all-gather.17
  528.9 60.6 all-gather.35
  592.3 60.6 all-gather.27
  655.6 60.6 all-gather.19
  718.8 145.5 all-gather.37
  866.8 144.4 all-gather.29
  1013.8 144.4 all-gather.21
  1184.7 82.6 reduce-scatter.1
  1270.0 189.3 all-reduce.3
  1462.3 154.3 all-reduce.5
where the time goes:
time: 1780 us; the launch traced here: 1770 us
  waiting for transfers between devices  1430 us (80%)
  matrix products  144 us (8%)
  other arithmetic  123 us (7%)
  local copies, waits for them, and re-layouts  50.4 us (3%)
  between operations  18.9 us (1%)
    all_gather x9, waiting for transfers between devices, body(): lax.all_gather(approx, ('row', 'col'), axis=0, tiled=True)  458 us
    all_gather x3, waiting for transfers between devices, body(): lax.all_gather(solved, ('row', 'col'), axis=1, tiled=True)  388 us
    psum x1, waiting for transfers between devices, body(): panel_rows = lax.psum(matmul(schur, select_cols), ('row', 'col'))  189 us
    psum x1, waiting for transfers between devices, body(): block = lax.psum(matmul(select_rows, panel_rows), 'scen')  154 us
    all_gather x1, waiting for transfers between devices, body(): kkt_all = lax.all_gather(kkt, ('row', 'col'), axis=1, tiled=True)  103 us
    reduce_scatter x1, waiting for transfers between devices, body(): lax.psum_scatter(tile_total, 'scen', scatter_dimension=0, tiled=True)  82.1 us
    another operation x15, other arithmetic, body(): lower_factor = jnp.linalg.cholesky(symmetric)  79.6 us
    dot_general x3, matrix products, contract(): lax.dot_general(left, right, (((0,), (0,)), ((), ())), precision=HIGH, pr...  75.2 us
  transfers between devices with their start and end apart: 17, of which 17 were waited for; matrix products, arithmetic and copies ran while one was open for 6% of the time, Pallas kernels for 0%

commit v1 on v0

v1 whole, which is shorter than its diff:
```python
import jax
import jax.numpy as jnp
from jax import lax
from jax.sharding import PartitionSpec as P

AXES = ("scen", "row", "col")
HIGH = lax.Precision.HIGH
HIGHEST = lax.Precision.HIGHEST
HORNER = 7


def place(device):
    scen, rest = divmod(device, 16)
    r, c = divmod(rest, 8)
    return (scen // 4, scen % 4, r, c // 2, c % 2)


def number(zl, x, r, y, h):
    return ((zl % 4) * 4 + x % 4) * 16 + (r % 2) * 8 + (y % 4) * 2 + h % 2


def block_of(r, y, h):
    return (r % 2) * 8 + (y % 4) * 2 + h % 2


def send(value, where):
    pairs = []
    for device in range(256):
        target = where(*place(device))
        if target is not None:
            pairs.append((device, target))
    return lax.ppermute(value, AXES, pairs)


def to_core(zl, x, r, y, h):
    return number(zl, x, r + 1, y, h)


def to_far(zl, x, r, y, h):
    return number(zl, x, r, y, h + 1)


def to_y(step):
    return lambda zl, x, r, y, h: number(zl, x, r, y + step, h)


def to_x(step):
    return lambda zl, x, r, y, h: number(zl, x + step, r, y, h)


def to_z(step):
    return lambda zl, x, r, y, h: number(zl + step, x, r, y, h)


def to_pair(zl, x, r, y, h):
    return number(zl, x ^ 1, r, y, h)


def pick(array, index, axis=0):
    return lax.dynamic_index_in_dim(array, index, axis, keepdims=False)


def final_target(step):
    def where(zl, x, r, y, h):
        i = block_of
        f, e = divmod(zl, 2)
        t = (x - step) % 4
        if t < 3:
            row, col = i(r, y + t, h ^ f), i(r ^ e, y, h)
        else:
            col, row = i(r, y + 1, h ^ f), i(r ^ e, y, h)
        return row * 16 + col

    return where


def mirror_target(step):
    def where(zl, x, r, y, h):
        if x != step:
            return None
        f, e = divmod(zl, 2)
        col, row = block_of(r, y + 2, h ^ f), block_of(r ^ e, y, h)
        return row * 16 + col

    return where


def contract(left, right):
    return lax.dot_general(
        left, right, (((0,), (0,)), ((), ())), precision=HIGH, preferred_element_type=jnp.float32
    )


def contract_all(left, right):
    return sum(contract(left[slot], right[slot]) for slot in range(left.shape[0]))


def reduce_pieces(parts, axis_index, step_of):
    total = pick(parts, axis_index)
    for step in (1, 2, 3):
        total = total + send(pick(parts, (axis_index + step) % 4), step_of(step))
    return total


def gather_pieces(piece, axis_index, step_of):
    got = [piece] + [send(piece, step_of(step)) for step in (1, 2, 3)]
    ring = jnp.stack([got[0], got[3], got[2], got[1]])
    return lax.dynamic_slice_in_dim(jnp.concatenate([ring, ring]), (4 - axis_index) % 4, 4, 0)


def gather_kkt(rows, x, r, y, h):
    far = send(rows, to_far)
    slots, count, order = rows.shape

    def around(piece):
        up = send(piece, to_y(1))
        down = send(piece, to_y(-1))
        half = count // 2
        across = jnp.concatenate(
            [send(up[:, :half], to_y(1)), send(down[:, half:], to_y(-1))], axis=1
        )
        ring = jnp.stack([piece, down, across, up], axis=1)
        return lax.dynamic_slice_in_dim(
            jnp.concatenate([ring, ring], axis=1), (4 - y) % 4, 4, 1
        )

    own, other = around(rows), around(far)
    both = jnp.where(h == 0, jnp.stack([own, other], 2), jnp.stack([other, own], 2))
    core = send(both, to_core)
    everything = jnp.where(r == 0, jnp.stack([both, core], 1), jnp.stack([core, both], 1))
    return everything.reshape(slots, 16 * count, order)


def solve(kkt_full, border):
    inv_diag = (1.0 / jnp.diagonal(kkt_full, axis1=1, axis2=2))[:, :, None]
    solved = inv_diag * border
    for step in range(HORNER):
        product = lax.dot_general(
            kkt_full, solved, (((2,), (1,)), ((0,), (0,))), precision=HIGH,
            preferred_element_type=jnp.float32,
        )
        solved = solved + inv_diag * (border - product)
    return solved


def body(kkt, border, first_diag, assignment, panel):
    scen_index = lax.axis_index("scen")
    own_index = lax.axis_index(("row", "col"))
    zl, x = scen_index // 4, scen_index % 4
    r, y, h = own_index // 8, (own_index // 2) % 4, own_index % 2
    slots, order, width = border.shape
    quarter = width // 4
    first, last = 2 * h, 2 - 2 * h
    lead = 2 * (y // 2)

    far_first = send(pick(border, last), to_far)
    own_one = send(border, to_y(-1))
    own_two = send(send(pick(border, 2 - lead), to_y(1)), to_y(1))

    swapped = send(kkt, to_pair)
    ids = scen_index * slots + jnp.arange(slots, dtype=jnp.int32)
    rows = jnp.where((assignment == ids)[:, None, None], kkt, swapped)
    kkt_full = gather_kkt(rows, x, r, y, h)

    far_mid = send(border[1], to_far)
    far_last = send(pick(border, first), to_far)
    far_first_one = send(far_first, to_y(-1))
    far_two = send(send(far_first, to_y(1)), to_y(1))
    far_mid_one = send(far_mid, to_y(-1))
    shared = jnp.where(y < 2, far_mid, border[1])
    shared_two = send(send(shared, to_y(1)), to_y(1))
    far_last_one = send(far_last, to_y(-1))

    solved = solve(kkt_full, border)
    other = send(solved, to_core)
    wide = jnp.concatenate([solved, other], axis=2)

    eye = jnp.eye(width, dtype=jnp.float32)
    diag = jnp.where(scen_index == own_index, eye * first_diag[:, None], 0.0)

    own_tile = contract_all(border, solved) + diag
    off_tile = contract(far_first, pick(solved, first))
    off_tile = off_tile + jnp.where(h == 0, contract(far_mid, solved[1]), 0.0)
    corner = jnp.stack([own_tile, off_tile]).reshape(2, 4, 4, quarter // 4, width)
    corner = corner.transpose(1, 2, 0, 3, 4)
    corner = reduce_pieces(corner, x, to_x)
    corner = reduce_pieces(corner, zl, to_z)
    corner = jnp.stack([corner, send(corner, to_far)])
    corner = gather_pieces(corner, zl, to_z)
    corner = gather_pieces(corner, x, to_x)
    corner = corner.transpose(2, 3, 0, 1, 4, 5).reshape(2, 2, width, width)
    cross = corner[0, 1] + corner[1, 1].T
    lower_left = jnp.where(h == 0, cross, cross.T)
    upper_left = jnp.where(h == 0, corner[0, 0], corner[1, 0])
    lower_right = jnp.where(h == 0, corner[1, 0], corner[0, 0])
    block = jnp.concatenate(
        [
            jnp.concatenate([upper_left, lower_left.T], axis=1),
            jnp.concatenate([lower_left, lower_right], axis=1),
        ],
        axis=0,
    )
    symmetric = 0.5 * (block + block.T)
    lower_factor = jnp.linalg.cholesky(symmetric)
    inverse = lax.linalg.triangular_solve(
        lower_factor, jnp.eye(2 * width, dtype=jnp.float32), left_side=True, lower=True
    )
    inverse_cols = lax.dynamic_slice_in_dim(inverse, h * width, width, 1)

    wide_first, wide_last = pick(wide, first), pick(wide, last)

    def reduced(own, partner):
        parts = jnp.stack([own, partner]).reshape(2, 4, quarter, 2, width)
        parts = parts.transpose(1, 0, 3, 2, 4).reshape(4, 4, quarter, width)
        return reduce_pieces(reduce_pieces(parts, x, to_x), zl, to_z)

    beside = contract_all(border, other)
    piece_zero = reduced(
        jnp.concatenate([own_tile, beside], axis=1),
        contract(far_first, wide_first) + contract(far_mid, wide[1]) + contract(far_last, wide_last),
    )
    common = contract(shared_two, wide[1])
    piece_two = reduced(
        contract(own_two, pick(wide, lead)) + jnp.where(y < 2, common, 0.0),
        contract(far_two, wide_first) + jnp.where(y < 2, 0.0, common),
    )
    piece_one = reduced(
        contract_all(own_one, wide),
        contract(far_first_one, wide_first)
        + contract(far_mid_one, wide[1])
        + contract(far_last_one, wide_last),
    )
    pieces = jnp.stack([piece_zero, piece_one, piece_two, piece_one])
    got = [send(pick(pieces, (x - step) % 4), final_target(step)) for step in range(4)]
    mirrored = [send(piece_two, mirror_target(step)) for step in range(4)]
    distance = ((scen_index // 2) % 4 - y) % 4
    ring = jnp.concatenate(got + got, axis=0)
    tile = lax.dynamic_slice_in_dim(ring, ((4 - distance) % 4) * quarter, width, 0)
    schur = jnp.where(distance == 3, tile.T, tile) + jnp.concatenate(mirrored, axis=0).T

    share = 2 * width // 16
    term = lax.dot_general(
        inverse_cols, schur, (((1,), (1,)), ((), ())), precision=HIGHEST,
        preferred_element_type=jnp.float32,
    )
    term = jnp.where(own_index // 2 == panel[0], term, 0.0).reshape(16, share, width)
    shares = lax.all_to_all(term, ("row", "col"), 0, 0, tiled=True)
    chosen = lax.dynamic_slice_in_dim(shares, 2 * panel[0], 2, 0)
    return (schur, (chosen[0] + chosen[1]).T)


def solution(mesh):
    in_specs = (
        P("scen", ("row", "col"), None),
        P("scen", None, ("row", "col")),
        P("scen"),
        P("scen"),
        P(),
    )
    out_specs = (P("scen", ("row", "col")), P("scen", ("row", "col")))
    return jax.shard_map(body, mesh=mesh, in_specs=in_specs, out_specs=out_specs, check_vma=False)
```

time: 1780 us -> 657 us (0.37)
  waiting for transfers between devices: 1430 us -> 138 us
  starting transfers between devices: 2.8 us -> 136 us
  other arithmetic: 123 us -> 158 us
  local copies, waits for them, and re-layouts: 50.4 us -> 78.2 us
    all_gather x13 -> x0, waiting for transfers between devices: 950 us -> none  [the longest x9 458 us: body(): lax.all_gather(approx, ('row', 'col'), axis=0, tiled=True)]
    psum x2 -> x0, waiting for transfers between devices: 344 us -> none  [the longest x1 189 us: body(): panel_rows = lax.psum(matmul(schur, select_cols), ('row', 'col'))]
    ppermute x1 -> x64, starting transfers between devices: 1.55 us -> 119 us  [send(): return lax.ppermute(value, AXES, pairs)]
    reduce_scatter x1 -> x0, waiting for transfers between devices: 82.1 us -> none  [body(): lax.psum_scatter(tile_total, 'scen', scatter_dimension=0, tiled=True)]
    ppermute x1 -> x64, waiting for transfers between devices: 50.8 us -> 118 us  [send(): return lax.ppermute(value, AXES, pairs)]
    dot_general x3 -> x20, matrix products: 75.2 us -> 49.8 us  [contract(): lax.dot_general(left, right, (((0,), (0,)), ((), ())), precision=HIGH, pr...]
    gather x3 -> x1, local copies, waits for them, and re-layouts: 31.1 us -> 7.45 us  [solve(): inv_diag = (1.0 / jnp.diagonal(kkt_full, axis1=1, axis2=2))[:, :, None]]
    all_to_all x0 -> x1, waiting for transfers between devices: none -> 19.7 us  [body(): shares = lax.all_to_all(term, ('row', 'col'), 0, 0, tiled=True)]
  transfers between devices with their start and end apart: 17 -> 65, of which waited for: 17 -> 30; matrix products, arithmetic and copies ran while one was open for 6% -> 55% of each run, Pallas kernels for 0% -> 0%
where the time goes in v1:
time: 657 us; the launch traced here: 645 us
  other arithmetic  158 us (24%)
  waiting for transfers between devices  138 us (21%)
  starting transfers between devices  136 us (21%)
  matrix products  130 us (20%)
  local copies, waits for them, and re-layouts  78.2 us (12%)
    ppermute x64, starting transfers between devices, send(): return lax.ppermute(value, AXES, pairs)  119 us
    ppermute x64, waiting for transfers between devices, send(): return lax.ppermute(value, AXES, pairs)  118 us
    another operation x14, other arithmetic, body(): lower_factor = jnp.linalg.cholesky(symmetric)  83.4 us
    dot_general x7, matrix products, solve(): lax.dot_general(kkt_full, solved, (((2,), (1,)), ((0,), (0,))), precision...  62.2 us
    dot_general x20, matrix products, contract(): lax.dot_general(left, right, (((0,), (0,)), ((), ())), precision=HIGH, pr...  49.8 us
    another operation x3, other arithmetic, body(): lax.linalg.triangular_solve(lower_factor, jnp.eye(2 * width, dtype=jnp.fl...  41.2 us
    all_to_all x1, waiting for transfers between devices, body(): shares = lax.all_to_all(term, ('row', 'col'), 0, 0, tiled=True)  19.7 us
    all_to_all x1, starting transfers between devices, body(): shares = lax.all_to_all(term, ('row', 'col'), 0, 0, tiled=True)  17.9 us
  transfers between devices with their start and end apart: 65, of which 30 were waited for; matrix products, arithmetic and copies ran while one was open for 55% of the time, Pallas kernels for 0%

profile of v1, /device:TPU:32, one launch (start us, length us, event | category | flops | bytes accessed | tf_op | source)
XLA Modules:
  0.0 645.4 jit_solution(9371840170013021221)
XLA Ops:
  2.9 10.0 %collective-permute-done = f32[3,48,768]{2,1,0:T(8,128)S(1)} collective-permute-done((f32[3,48,768]{2,1,0:T(8,128)}, f32[3,48,768]{2,1,0:T(8,128)S(1)}, u32[]{:S(2)}, u32[]{:S(2)}) %collective-permute-start) | collective-permute-done | bytes 442400 | tf_op jit(solution)/shard_map/ppermute | solution.py:32
  18.0 6.3 collective-permute-start.5
  30.5 12.1 %collective-permute-done.5 = f32[3,48,768]{2,1,0:T(8,128)S(1)} collective-permute-done((f32[3,48,768]{2,1,0:T(8,128)S(1)}, f32[3,48,768]{2,1,0:T(8,128)S(1)}, u32[]{:S(2)}, u32[]{:S(2)}) %collective-permute-start.5) | collective-permute-done | bytes 442400 | tf_op jit(solution)/shard_map/ppermute | solution.py:32
  55.4 3.3 collective-permute-start.9
  58.7 3.8 collective-permute-done.8
  65.0 3.3 collective-permute-start.21
  68.3 3.7 dynamic-slice_bitcast_fusion.3
  72.0 5.9 collective-permute-start.13
  78.0 6.1 collective-permute-start.14
  87.5 6.2 maximum_select_fusion
  93.7 11.6 %copy.136 = f32[3,2,4,2,48,768]{5,0,4,3,2,1:T(4,128)} copy(f32[3,2,4,2,48,768]{5,4,2,0,3,1:T(8,128)} %maximum_select_fusion) | data formatting | bytes 14155776 | tf_op jit(solution)/shard_map/jit(_where)/select_n | solution.py:130
  105.3 7.5 %gather_fusion = f32[768,3]{0,1:T(4,128)S(1)} fusion(f32[3,768,768]{2,0,1:T(4,128)} %bitcast.418, s32[768]{0:T(1024)S(1)} %or_reduce_fusion), kind=kCustom, calls=%fused_computation | custom fusion | bytes 24576 | tf_op jit(solution)/shard_map/jit(diagonal)/gather | solution.py:135
  112.8 9.5 %multiply_add_fusion.6 = f32[3,768,256]{1,2,0:T(8,128)S(1)} fusion(f32[3,768,256]{1,2,0:T(8,128)} %copy.137, f32[3,768]{1,0:T(4,128)S(1)} %divide_bitcast_fusion, f32[3,768,768]{2,0,1:T(4,128)} %bitcast.419), kind=kOutput, calls=%fused_computation.24 | convolution fusion | flops 2720858112 | bytes 11805696 | tf_op jit(solution)/shard_map/dot_general | solution.py:138
  123.8 5.5 fusion.147
  129.3 11.0 %multiply_add_fusion.4 = f32[3,768,256]{1,2,0:T(8,128)} fusion(f32[3,768,256]{1,2,0:T(8,128)} %copy.137, f32[3,768,256]{1,2,0:T(8,128)} %copy-done.4, f32[3,768,256]{1,2,0:T(8,128)} %fusion.147, f32[3,768]{1,0:T(4,128)S(1)} %divide_bitcast_fusion, f32[3,768,768]{2,0,1:T(4,128)S(1)} %bitcast.423), kind=kOutput, calls=%fused_computation.22 | convolution fusion | flops 2723217408 | bytes 16524288 | tf_op jit(solution)/shard_map/dot_general | solution.py:138
  140.3 7.0 %fusion.144 = f32[3,768,256]{1,2,0:T(8,128)} fusion(f32[3,768,256]{1,2,0:T(8,128)} %multiply_add_fusion.4, f32[3,768,768]{2,0,1:T(4,128)S(1)} %bitcast.424), kind=kOutput, calls=%fused_computation.326 | convolution fusion | flops 2717908992 | bytes 11796480 | tf_op jit(solution)/shard_map/dot_general | solution.py:138
  147.3 11.1 %multiply_add_fusion.2 = f32[3,768,256]{1,2,0:T(8,128)} fusion(f32[3,768,256]{1,2,0:T(8,128)} %copy.137, f32[3,768,256]{1,2,0:T(8,128)} %multiply_add_fusion.4, f32[3,768,256]{1,2,0:T(8,128)} %fusion.144, f32[3,768]{1,0:T(4,128)S(1)} %divide_bitcast_fusion, f32[3,768,768]{2,0,1:T(4,128)S(1)} %bitcast.425), kind=kOutput, calls=%fused_computation.20 | convolution fusion | flops 2723217408 | bytes 16524288 | tf_op jit(solution)/shard_map/dot_general | solution.py:138
  158.4 7.3 %fusion.141 = f32[3,768,256]{1,2,0:T(8,128)} fusion(f32[3,768,256]{1,2,0:T(8,128)} %multiply_add_fusion.2, f32[3,768,768]{2,0,1:T(4,128)S(1)} %bitcast.426), kind=kOutput, calls=%fused_computation.323 | convolution fusion | flops 2717908992 | bytes 11796480 | tf_op jit(solution)/shard_map/dot_general | solution.py:138
  165.7 10.8 %multiply_add_fusion = f32[3,768,256]{1,2,0:T(8,128)} fusion(f32[3,768,256]{1,2,0:T(8,128)} %copy.137, f32[3,768,256]{1,2,0:T(8,128)} %multiply_add_fusion.2, f32[3,768,256]{1,2,0:T(8,128)} %fusion.141, f32[3,768]{1,0:T(4,128)S(1)} %divide_bitcast_fusion, f32[3,768,768]{2,0,1:T(4,128)S(1)} %bitcast.427), kind=kOutput, calls=%fused_computation.18 | convolution fusion | flops 2723217408 | bytes 16524288 | tf_op jit(solution)/shard_map/dot_general | solution.py:138
  204.3 7.3 %collective-permute-done.57 = f32[2,16,256]{2,1,0:T(8,128)S(1)} collective-permute-done((f32[2,16,256]{2,1,0:T(8,128)S(1)}, f32[2,16,256]{2,1,0:T(8,128)S(1)}, u32[]{:S(2)}, u32[]{:S(2)}) %collective-permute-start.57) | collective-permute-done | bytes 32800 | tf_op jit(solution)/shard_map/ppermute | solution.py:32
  226.9 3.6 collective-permute-done.61
  233.4 5.1 collective-permute-done.63
  256.4 11.7 %cholesky.104 = f32[128,128]{1,0:T(8,128)S(1)} custom-call(f32[128,128]{1,0:T(8,128)S(1)} %cholesky.266), custom_call_target="Cholesky" | custom-call | tf_op jit(solution)/shard_map/jit(cholesky)/cholesky | solution.py:204
  268.2 9.8 %custom-call.30 = f32[1,128,128]{1,2,0:T(8,128)S(1)} custom-call(f32[1,128,128]{2,1,0:T(8,128)S(1)} %get-tuple-element.79), custom_call_target="InvertDiagBlocksLowerTriangular" | custom-call | tf_op jit(solution)/shard_map/jit(cholesky)/cholesky | solution.py:204
  281.3 11.9 %cholesky.217 = f32[128,128]{1,0:T(8,128)S(1)} custom-call(f32[128,128]{1,0:T(8,128)S(1)} %cholesky.270), custom_call_target="Cholesky" | custom-call | tf_op jit(solution)/shard_map/jit(cholesky)/cholesky | solution.py:204
  293.2 9.8 %custom-call.31 = f32[1,128,128]{1,2,0:T(8,128)S(1)} custom-call(f32[1,128,128]{2,1,0:T(8,128)S(1)} %get-tuple-element.76), custom_call_target="InvertDiagBlocksLowerTriangular" | custom-call | tf_op jit(solution)/shard_map/jit(cholesky)/cholesky | solution.py:204
  306.1 13.2 %cholesky.238 = f32[128,128]{1,0:T(8,128)} custom-call(f32[128,128]{1,0:T(8,128)} %cholesky.275), custom_call_target="Cholesky" | custom-call | tf_op jit(solution)/shard_map/jit(cholesky)/cholesky | solution.py:204
  321.4 11.3 %custom-call.32 = f32[1,128,128]{1,2,0:T(8,128)} custom-call(f32[1,128,128]{2,1,0:T(8,128)} %get-tuple-element.73), custom_call_target="InvertDiagBlocksLowerTriangular" | custom-call | tf_op jit(solution)/shard_map/jit(cholesky)/cholesky | solution.py:204
  335.0 12.1 %cholesky.255 = f32[128,128]{1,0:T(8,128)S(1)} custom-call(f32[128,128]{1,0:T(8,128)S(1)} %convolution_subtract_fusion.5), custom_call_target="Cholesky" | custom-call | tf_op jit(solution)/shard_map/jit(cholesky)/cholesky | solution.py:204
  352.1 13.6 %while.1 = (s32[]{:T(128)}, f32[512,512]{1,0:T(8,128)}, s32[4,2]{0,1:T(2,128)S(1)}, f32[4,128,128]{2,1,0:T(8,128)}, s32[]{:T(128)}) while((s32[]{:T(128)}, f32[512,512]{1,0:T(8,128)}, s32[4,2]{0,1:T(2,128)S(1)}, f32[4,128,128]{2,1,0:T(8,128)}, s32[]{:T(128)}) %tuple.65), condition=%wide.while_cond, body=%wide.while_body.sunk | while | flops 2 | bytes 132705 | solution.py:205
  365.7 40.1 %custom-call.33 = f32[4,128,128]{1,2,0:T(8,128)S(1)} custom-call(f32[4,128,128]{2,1,0:T(8,128)} %get-tuple-element.9), custom_call_target="InvertDiagBlocksLowerTriangular" | custom-call | tf_op jit(solution)/shard_map/triangular_solve | solution.py:205
  426.6 4.0 fusion.138
  432.6 3.5 fusion.23
  466.0 3.5 collective-permute-done.22
  476.6 17.3 %collective-permute-done.34 = f32[768,256]{1,0:T(8,128)} collective-permute-done((f32[768,256]{1,0:T(8,128)}, f32[768,256]{1,0:T(8,128)}, u32[]{:S(2)}, u32[]{:S(2)}) %collective-permute-start.34) | collective-permute-done | bytes 786464 | tf_op jit(solution)/shard_map/ppermute | solution.py:32
  498.6 3.6 fusion.33
  504.6 5.4 collective-permute-done.36
  511.2 3.4 convolution_add_fusion
  529.4 4.0 collective-permute-start.19
  540.0 3.9 collective-permute-start.29
  549.7 3.4 collective-permute-done.29
  553.1 6.6 %collective-permute-done.30 = f32[64,256]{0,1:T(8,128)S(1)} collective-permute-done((f32[64,256]{0,1:T(8,128)S(1)}, f32[64,256]{0,1:T(8,128)S(1)}, u32[]{:S(2)}, u32[]{:S(2)}) %collective-permute-start.30) | collective-permute-done | bytes 65568 | tf_op jit(solution)/shard_map/ppermute | solution.py:32
  567.8 6.6 %collective-permute-start.47 = (f32[64,256]{0,1:T(8,128)S(1)}, f32[64,256]{0,1:T(8,128)S(1)}, u32[]{:S(2)}, u32[]{:S(2)}) collective-permute-start(f32[64,256]{0,1:T(8,128)S(1)} %fusion.108), channel_id=1, source_target_pairs={{0,4},{1,21},{2,38},{3,55},{4,64},{5,81},{6,98},{7,115},{8,140},{9... | collective-permute-start | bytes 196616 | tf_op jit(solution)/shard_map/ppermute | solution.py:32
  580.6 6.3 collective-permute-done.44
  588.8 4.2 collective-permute-done.45
  593.1 10.1 %collective-permute-start.46 = (f32[64,256]{1,0:T(8,128)S(1)}, f32[64,256]{1,0:T(8,128)S(1)}, u32[]{:S(2)}, u32[]{:S(2)}) collective-permute-start(f32[64,256]{1,0:T(8,128)S(1)} %bitcast.457), channel_id=1, source_target_pairs={{0,32},{1,49},{2,66},{3,83},{4,100},{5,117},{6,6},{7,23},{8,168},{... | collective-permute-start | bytes 196616 | tf_op jit(solution)/shard_map/ppermute | solution.py:32
  606.9 17.9 %all-to-all-start = ((f32[16,32,256]{2,1,0:T(8,128)}), f32[16,32,256]{2,1,0:T(8,128)S(1)}, u32[]{:S(2)}, u32[]{:S(2)}) async-start(f32[16,32,256]{2,1,0:T(8,128)} %bitcast.147), calls=%async_computation | async-start | bytes 1048576 | tf_op jit(solution)/shard_map/all_to_all | solution.py:247
  624.9 19.7 %all-to-all-done = f32[16,32,256]{2,1,0:T(8,128)S(1)} async-done(((f32[16,32,256]{2,1,0:T(8,128)}), f32[16,32,256]{2,1,0:T(8,128)S(1)}, u32[]{:S(2)}, u32[]{:S(2)}) %all-to-all-start) | async-done | bytes 524320 | tf_op jit(solution)/shard_map/all_to_all | solution.py:247
  (350 shorter events, 239.4 us)
Async XLA Ops:
  0.6 12.2 %collective-permute-start = (f32[3,48,768]{2,1,0:T(8,128)}, f32[3,48,768]{2,1,0:T(8,128)S(1)}, u32[]{:S(2)}, u32[]{:S(2)}) collective-permute-start(f32[3,48,768]{2,1,0:T(8,128)} %param.5), channel_id=1, source_target_pairs={{0,16},{1,17},{2,18},{3,19},{4,20},{5,21},{6,22},{7,23},{8,24},{9,... | collective-permute-start | bytes 1327112 | tf_op jit(solution)/shard_map/ppermute | solution.py:32
  14.7 12.3 %collective-permute-start.2 = (f32[3,48,768]{2,1,0:T(8,128)S(1)}, f32[3,48,768]{2,1,0:T(8,128)S(1)}, u32[]{:S(2)}, u32[]{:S(2)}) collective-permute-start(f32[3,48,768]{2,1,0:T(8,128)S(1)} %get-tuple-element.21), channel_id=1, source_target_pairs={{0,2},{1,3},{2,4},{3,5},{4,6},{5,7},{6,0},{7,1},{8,10},{9,11},{10,... | collective-permute-start | bytes 1327112 | tf_op jit(solution)/shard_map/ppermute | solution.py:32
  16.3 11.1 %collective-permute-start.1 = (f32[3,48,768]{2,1,0:T(8,128)S(1)}, f32[3,48,768]{2,1,0:T(8,128)S(1)}, u32[]{:S(2)}, u32[]{:S(2)}) collective-permute-start(f32[3,48,768]{2,1,0:T(8,128)S(1)} %get-tuple-element.21), channel_id=1, source_target_pairs={{0,6},{1,7},{2,0},{3,1},{4,2},{5,3},{6,4},{7,5},{8,14},{9,15},{10,... | collective-permute-start | bytes 1327112 | tf_op jit(solution)/shard_map/ppermute | solution.py:32
  18.0 24.6 %collective-permute-start.5 = (f32[3,48,768]{2,1,0:T(8,128)S(1)}, f32[3,48,768]{2,1,0:T(8,128)S(1)}, u32[]{:S(2)}, u32[]{:S(2)}) collective-permute-start(f32[3,48,768]{2,1,0:T(8,128)S(1)} %get-tuple-element.21), channel_id=1, source_target_pairs={{0,1},{1,0},{2,3},{3,2},{4,5},{5,4},{6,7},{7,6},{8,9},{9,8},{10,11... | collective-permute-start | bytes 1327112 | tf_op jit(solution)/shard_map/ppermute | solution.py:32
  27.1 18.5 %collective-permute-start.3 = (f32[3,24,768]{2,1,0:T(8,128)S(1)}, f32[3,24,768]{2,1,0:T(8,128)S(1)}, u32[]{:S(2)}, u32[]{:S(2)}) collective-permute-start(f32[3,24,768]{2,1,0:T(8,128)S(1)} %slice.232), channel_id=1, source_target_pairs={{0,2},{1,3},{2,4},{3,5},{4,6},{5,7},{6,0},{7,1},{8,10},{9,11},{10,... | collective-permute-start | bytes 663560 | tf_op jit(solution)/shard_map/ppermute | solution.py:32
  27.5 18.1 %collective-permute-start.4 = (f32[3,24,768]{2,1,0:T(8,128)S(1)}, f32[3,24,768]{2,1,0:T(8,128)S(1)}, u32[]{:S(2)}, u32[]{:S(2)}) collective-permute-start(f32[3,24,768]{2,1,0:T(8,128)S(1)} %slice.233), channel_id=1, source_target_pairs={{0,6},{1,7},{2,0},{3,1},{4,2},{5,3},{6,4},{7,5},{8,14},{9,15},{10,... | collective-permute-start | bytes 663560 | tf_op jit(solution)/shard_map/ppermute | solution.py:32
  42.6 12.7 %collective-permute-start.6 = (f32[3,48,768]{2,1,0:T(8,128)S(1)}, f32[3,48,768]{2,1,0:T(8,128)S(1)}, u32[]{:S(2)}, u32[]{:S(2)}) collective-permute-start(f32[3,48,768]{2,1,0:T(8,128)S(1)} %collective-permute-done.5), channel_id=1, source_target_pairs={{0,6},{1,7},{2,0},{3,1},{4,2},{5,3},{6,4},{7,5},{8,14},{9,15},{10,... | collective-permute-start | bytes 1327112 | tf_op jit(solution)/shard_map/ppermute | solution.py:32
  44.4 10.8 %collective-permute-start.7 = (f32[3,48,768]{2,1,0:T(8,128)S(1)}, f32[3,48,768]{2,1,0:T(8,128)S(1)}, u32[]{:S(2)}, u32[]{:S(2)}) collective-permute-start(f32[3,48,768]{2,1,0:T(8,128)S(1)} %collective-permute-done.5), channel_id=1, source_target_pairs={{0,2},{1,3},{2,4},{3,5},{4,6},{5,7},{6,0},{7,1},{8,10},{9,11},{10,... | collective-permute-start | bytes 1327112 | tf_op jit(solution)/shard_map/ppermute | solution.py:32
  65.0 22.5 %collective-permute-start.10 = (f32[3,4,2,48,768]{4,3,1,0,2:T(8,128)}, f32[3,4,2,48,768]{4,3,1,0,2:T(8,128)}, u32[]{:S(2)}, u32[]{:S(2)}) collective-permute-start(f32[3,4,2,48,768]{4,3,1,0,2:T(8,128)} %maximum_select_fusion.2), channel_id=1, source_target_pairs={{0,8},{1,9},{2,10},{3,11},{4,12},{5,13},{6,14},{7,15},{8,0},{9,1},... | collective-permute-start | bytes 10616840 | tf_op jit(solution)/shard_map/ppermute | solution.py:32
  65.0 373.3 %collective-permute-start.21 = (f32[3,768,256]{2,1,0:T(8,128)}, f32[3,768,256]{2,1,0:T(8,128)}, u32[]{:S(2)}, u32[]{:S(2)}) collective-permute-start(f32[3,768,256]{2,1,0:T(8,128)} %param.6), channel_id=1, source_target_pairs={{0,6},{1,7},{2,0},{3,1},{4,2},{5,3},{6,4},{7,5},{8,14},{9,15},{10,... | collective-permute-start | bytes 7077896 | tf_op jit(solution)/shard_map/ppermute | solution.py:32
  72.0 106.8 %collective-permute-start.13 = (f32[768,256]{1,0:T(8,128)}, f32[768,256]{1,0:T(8,128)}, u32[]{:S(2)}, u32[]{:S(2)}) collective-permute-start(f32[768,256]{1,0:T(8,128)} %get-tuple-element.29), channel_id=1, source_target_pairs={{0,1},{1,0},{2,3},{3,2},{4,5},{5,4},{6,7},{7,6},{8,9},{9,8},{10,11... | collective-permute-start | bytes 2359304 | tf_op jit(solution)/shard_map/ppermute | solution.py:32
  77.9 102.8 %collective-permute-start.12 = (f32[768,256]{1,0:T(8,128)}, f32[768,256]{1,0:T(8,128)}, u32[]{:S(2)}, u32[]{:S(2)}) collective-permute-start(f32[768,256]{1,0:T(8,128)} %get-tuple-element.30), channel_id=1, source_target_pairs={{0,1},{1,0},{2,3},{3,2},{4,5},{5,4},{6,7},{7,6},{8,9},{9,8},{10,11... | collective-permute-start | bytes 2359304 | tf_op jit(solution)/shard_map/ppermute | solution.py:32
  78.0 336.1 %collective-permute-start.14 = (f32[768,256]{1,0:T(8,128)}, f32[768,256]{1,0:T(8,128)}, u32[]{:S(2)}, u32[]{:S(2)}) collective-permute-start(f32[768,256]{1,0:T(8,128)} %get-tuple-element.28), channel_id=1, source_target_pairs={{0,1},{1,0},{2,3},{3,2},{4,5},{5,4},{6,7},{7,6},{8,9},{9,8},{10,11... | collective-permute-start | bytes 2359304 | tf_op jit(solution)/shard_map/ppermute | solution.py:32
  201.1 249.0 %collective-permute-start.31 = (f32[768,256]{1,0:T(8,128)}, f32[768,256]{1,0:T(8,128)}, u32[]{:S(2)}, u32[]{:S(2)}) collective-permute-start(f32[768,256]{1,0:T(8,128)} %get-tuple-element.31), channel_id=1, source_target_pairs={{0,2},{1,3},{2,4},{3,5},{4,6},{5,7},{6,0},{7,1},{8,10},{9,11},{10,... | collective-permute-start | bytes 2359304 | tf_op jit(solution)/shard_map/ppermute | solution.py:32
  233.4 222.4 %collective-permute-start.33 = (f32[768,256]{1,0:T(8,128)}, f32[768,256]{1,0:T(8,128)}, u32[]{:S(2)}, u32[]{:S(2)}) collective-permute-start(f32[768,256]{1,0:T(8,128)} %broadcast_select_fusion), channel_id=1, source_target_pairs={{0,2},{1,3},{2,4},{3,5},{4,6},{5,7},{6,0},{7,1},{8,10},{9,11},{10,... | collective-permute-start | bytes 2359304 | tf_op jit(solution)/shard_map/ppermute | solution.py:32
  238.6 176.5 %collective-permute-start.11 = (f32[3,768,256]{1,2,0:T(8,128)S(1)}, f32[3,768,256]{1,2,0:T(8,128)}, u32[]{:S(2)}, u32[]{:S(2)}) collective-permute-start(f32[3,768,256]{1,2,0:T(8,128)S(1)} %copy-done), channel_id=1, source_target_pairs={{0,8},{1,9},{2,10},{3,11},{4,12},{5,13},{6,14},{7,15},{8,0},{9,1},... | collective-permute-start | bytes 7077896 | tf_op jit(solution)/shard_map/ppermute | solution.py:32
  414.0 40.7 %collective-permute-start.23 = (f32[768,256]{1,0:T(8,128)}, f32[768,256]{1,0:T(8,128)}, u32[]{:S(2)}, u32[]{:S(2)}) collective-permute-start(f32[768,256]{1,0:T(8,128)} %collective-permute-done.13), channel_id=1, source_target_pairs={{0,6},{1,7},{2,0},{3,1},{4,2},{5,3},{6,4},{7,5},{8,14},{9,15},{10,... | collective-permute-start | bytes 2359304 | tf_op jit(solution)/shard_map/ppermute | solution.py:32
  415.1 47.8 %collective-permute-start.24 = (f32[768,256]{1,0:T(8,128)}, f32[768,256]{1,0:T(8,128)}, u32[]{:S(2)}, u32[]{:S(2)}) collective-permute-start(f32[768,256]{1,0:T(8,128)} %collective-permute-done.14), channel_id=1, source_target_pairs={{0,6},{1,7},{2,0},{3,1},{4,2},{5,3},{6,4},{7,5},{8,14},{9,15},{10,... | collective-permute-start | bytes 2359304 | tf_op jit(solution)/shard_map/ppermute | solution.py:32
  438.3 21.7 %collective-permute-start.35 = (f32[768,256]{1,0:T(8,128)}, f32[768,256]{1,0:T(8,128)}, u32[]{:S(2)}, u32[]{:S(2)}) collective-permute-start(f32[768,256]{1,0:T(8,128)} %collective-permute-done.12), channel_id=1, source_target_pairs={{0,2},{1,3},{2,4},{3,5},{4,6},{5,7},{6,0},{7,1},{8,10},{9,11},{10,... | collective-permute-start | bytes 2359304 | tf_op jit(solution)/shard_map/ppermute | solution.py:32
  450.2 19.3 %collective-permute-start.22 = (f32[768,256]{1,0:T(8,128)}, f32[768,256]{1,0:T(8,128)S(1)}, u32[]{:S(2)}, u32[]{:S(2)}) collective-permute-start(f32[768,256]{1,0:T(8,128)} %collective-permute-done.12), channel_id=1, source_target_pairs={{0,6},{1,7},{2,0},{3,1},{4,2},{5,3},{6,4},{7,5},{8,14},{9,15},{10,... | collective-permute-start | bytes 2359304 | tf_op jit(solution)/shard_map/ppermute | solution.py:32
  454.7 43.8 %collective-permute-start.32 = (f32[768,256]{1,0:T(8,128)}, f32[768,256]{1,0:T(8,128)}, u32[]{:S(2)}, u32[]{:S(2)}) collective-permute-start(f32[768,256]{1,0:T(8,128)} %collective-permute-done.31), channel_id=1, source_target_pairs={{0,2},{1,3},{2,4},{3,5},{4,6},{5,7},{6,0},{7,1},{8,10},{9,11},{10,... | collective-permute-start | bytes 2359304 | tf_op jit(solution)/shard_map/ppermute | solution.py:32
  455.8 38.1 %collective-permute-start.34 = (f32[768,256]{1,0:T(8,128)}, f32[768,256]{1,0:T(8,128)}, u32[]{:S(2)}, u32[]{:S(2)}) collective-permute-start(f32[768,256]{1,0:T(8,128)} %collective-permute-done.33), channel_id=1, source_target_pairs={{0,2},{1,3},{2,4},{3,5},{4,6},{5,7},{6,0},{7,1},{8,10},{9,11},{10,... | collective-permute-start | bytes 2359304 | tf_op jit(solution)/shard_map/ppermute | solution.py:32
  460.0 50.0 %collective-permute-start.36 = (f32[768,256]{1,0:T(8,128)}, f32[768,256]{1,0:T(8,128)}, u32[]{:S(2)}, u32[]{:S(2)}) collective-permute-start(f32[768,256]{1,0:T(8,128)} %collective-permute-done.35), channel_id=1, source_target_pairs={{0,2},{1,3},{2,4},{3,5},{4,6},{5,7},{6,0},{7,1},{8,10},{9,11},{10,... | collective-permute-start | bytes 2359304 | tf_op jit(solution)/shard_map/ppermute | solution.py:32
  462.9 53.3 %collective-permute-start.15 = (f32[4,64,256]{2,1,0:T(8,128)}, f32[4,64,256]{2,1,0:T(8,128)}, u32[]{:S(2)}, u32[]{:S(2)}) collective-permute-start(f32[4,64,256]{2,1,0:T(8,128)} %get-tuple-element.37), channel_id=1, source_target_pairs={{0,16},{1,17},{2,18},{3,19},{4,20},{5,21},{6,22},{7,23},{8,24},{9,... | collective-permute-start | bytes 786440 | tf_op jit(solution)/shard_map/ppermute | solution.py:32
  469.5 48.5 %collective-permute-start.16 = (f32[4,64,256]{2,1,0:T(8,128)}, f32[4,64,256]{2,1,0:T(8,128)}, u32[]{:S(2)}, u32[]{:S(2)}) collective-permute-start(f32[4,64,256]{2,1,0:T(8,128)} %get-tuple-element.39), channel_id=1, source_target_pairs={{0,32},{1,33},{2,34},{3,35},{4,36},{5,37},{6,38},{7,39},{8,40},{9,... | collective-permute-start | bytes 786440 | tf_op jit(solution)/shard_map/ppermute | solution.py:32
  493.9 25.0 %collective-permute-start.17 = (f32[4,64,256]{2,1,0:T(8,128)}, f32[4,64,256]{2,1,0:T(8,128)}, u32[]{:S(2)}, u32[]{:S(2)}) collective-permute-start(f32[4,64,256]{2,1,0:T(8,128)} %get-tuple-element.38), channel_id=1, source_target_pairs={{0,48},{1,49},{2,50},{3,51},{4,52},{5,53},{6,54},{7,55},{8,56},{9,... | collective-permute-start | bytes 786440 | tf_op jit(solution)/shard_map/ppermute | solution.py:32
  498.5 22.9 %collective-permute-start.25 = (f32[4,64,256]{2,1,0:T(8,128)}, f32[4,64,256]{2,1,0:T(8,128)}, u32[]{:S(2)}, u32[]{:S(2)}) collective-permute-start(f32[4,64,256]{2,1,0:T(8,128)} %get-tuple-element.40), channel_id=1, source_target_pairs={{0,16},{1,17},{2,18},{3,19},{4,20},{5,21},{6,22},{7,23},{8,24},{9,... | collective-permute-start | bytes 786440 | tf_op jit(solution)/shard_map/ppermute | solution.py:32
  510.0 16.5 %collective-permute-start.26 = (f32[4,64,256]{2,1,0:T(8,128)}, f32[4,64,256]{2,1,0:T(8,128)}, u32[]{:S(2)}, u32[]{:S(2)}) collective-permute-start(f32[4,64,256]{2,1,0:T(8,128)} %get-tuple-element.42), channel_id=1, source_target_pairs={{0,32},{1,33},{2,34},{3,35},{4,36},{5,37},{6,38},{7,39},{8,40},{9,... | collective-permute-start | bytes 786440 | tf_op jit(solution)/shard_map/ppermute | solution.py:32
  516.9 12.5 %collective-permute-start.27 = (f32[4,64,256]{2,1,0:T(8,128)S(1)}, f32[4,64,256]{2,1,0:T(8,128)S(1)}, u32[]{:S(2)}, u32[]{:S(2)}) collective-permute-start(f32[4,64,256]{2,1,0:T(8,128)S(1)} %copy-done.23), channel_id=1, source_target_pairs={{0,48},{1,49},{2,50},{3,51},{4,52},{5,53},{6,54},{7,55},{8,56},{9,... | collective-permute-start | bytes 786440 | tf_op jit(solution)/shard_map/ppermute | solution.py:32
  518.0 15.4 %collective-permute-start.37 = (f32[4,64,256]{2,1,0:T(8,128)S(1)}, f32[4,64,256]{2,1,0:T(8,128)}, u32[]{:S(2)}, u32[]{:S(2)}) collective-permute-start(f32[4,64,256]{2,1,0:T(8,128)S(1)} %get-tuple-element.43), channel_id=1, source_target_pairs={{0,16},{1,17},{2,18},{3,19},{4,20},{5,21},{6,22},{7,23},{8,24},{9,... | collective-permute-start | bytes 786440 | tf_op jit(solution)/shard_map/ppermute | solution.py:32
  518.9 14.5 %collective-permute-start.38 = (f32[4,64,256]{2,1,0:T(8,128)S(1)}, f32[4,64,256]{2,1,0:T(8,128)}, u32[]{:S(2)}, u32[]{:S(2)}) collective-permute-start(f32[4,64,256]{2,1,0:T(8,128)S(1)} %get-tuple-element.45), channel_id=1, source_target_pairs={{0,32},{1,33},{2,34},{3,35},{4,36},{5,37},{6,38},{7,39},{8,40},{9,... | collective-permute-start | bytes 786440 | tf_op jit(solution)/shard_map/ppermute | solution.py:32
  521.5 14.4 %collective-permute-start.39 = (f32[4,64,256]{2,1,0:T(8,128)S(1)}, f32[4,64,256]{2,1,0:T(8,128)}, u32[]{:S(2)}, u32[]{:S(2)}) collective-permute-start(f32[4,64,256]{2,1,0:T(8,128)S(1)} %get-tuple-element.44), channel_id=1, source_target_pairs={{0,48},{1,49},{2,50},{3,51},{4,52},{5,53},{6,54},{7,55},{8,56},{9,... | collective-permute-start | bytes 786440 | tf_op jit(solution)/shard_map/ppermute | solution.py:32
  526.5 18.0 %collective-permute-start.18 = (f32[64,256]{0,1:T(8,128)}, f32[64,256]{0,1:T(8,128)S(1)}, u32[]{:S(2)}, u32[]{:S(2)}) collective-permute-start(f32[64,256]{0,1:T(8,128)} %bitcast.46), channel_id=1, source_target_pairs={{0,64},{1,65},{2,66},{3,67},{4,68},{5,69},{6,70},{7,71},{8,72},{9,... | collective-permute-start | bytes 196616 | tf_op jit(solution)/shard_map/ppermute | solution.py:32
  529.4 15.3 %collective-permute-start.19 = (f32[64,256]{0,1:T(8,128)}, f32[64,256]{0,1:T(8,128)S(1)}, u32[]{:S(2)}, u32[]{:S(2)}) collective-permute-start(f32[64,256]{0,1:T(8,128)} %bitcast.47), channel_id=1, source_target_pairs={{0,128},{1,129},{2,130},{3,131},{4,132},{5,133},{6,134},{7,135},{8... | collective-permute-start | bytes 196616 | tf_op jit(solution)/shard_map/ppermute | solution.py:32
  533.4 13.2 %collective-permute-start.20 = (f32[64,256]{0,1:T(8,128)S(1)}, f32[64,256]{0,1:T(8,128)S(1)}, u32[]{:S(2)}, u32[]{:S(2)}) collective-permute-start(f32[64,256]{0,1:T(8,128)S(1)} %bitcast.449), channel_id=1, source_target_pairs={{0,192},{1,193},{2,194},{3,195},{4,196},{5,197},{6,198},{7,199},{8... | collective-permute-start | bytes 196616 | tf_op jit(solution)/shard_map/ppermute | solution.py:32
  537.4 11.0 %collective-permute-start.28 = (f32[64,256]{0,1:T(8,128)S(1)}, f32[64,256]{0,1:T(8,128)S(1)}, u32[]{:S(2)}, u32[]{:S(2)}) collective-permute-start(f32[64,256]{0,1:T(8,128)S(1)} %bitcast.451), channel_id=1, source_target_pairs={{0,64},{1,65},{2,66},{3,67},{4,68},{5,69},{6,70},{7,71},{8,72},{9,... | collective-permute-start | bytes 196616 | tf_op jit(solution)/shard_map/ppermute | solution.py:32
  540.0 13.0 %collective-permute-start.29 = (f32[64,256]{0,1:T(8,128)S(1)}, f32[64,256]{0,1:T(8,128)S(1)}, u32[]{:S(2)}, u32[]{:S(2)}) collective-permute-start(f32[64,256]{0,1:T(8,128)S(1)} %bitcast.450), channel_id=1, source_target_pairs={{0,128},{1,129},{2,130},{3,131},{4,132},{5,133},{6,134},{7,135},{8... | collective-permute-start | bytes 196616 | tf_op jit(solution)/shard_map/ppermute | solution.py:32
  544.5 15.1 %collective-permute-start.30 = (f32[64,256]{0,1:T(8,128)S(1)}, f32[64,256]{0,1:T(8,128)S(1)}, u32[]{:S(2)}, u32[]{:S(2)}) collective-permute-start(f32[64,256]{0,1:T(8,128)S(1)} %bitcast.452), channel_id=1, source_target_pairs={{0,192},{1,193},{2,194},{3,195},{4,196},{5,197},{6,198},{7,199},{8... | collective-permute-start | bytes 196616 | tf_op jit(solution)/shard_map/ppermute | solution.py:32
  544.7 15.6 %collective-permute-start.40 = (f32[64,256]{0,1:T(8,128)S(1)}, f32[64,256]{0,1:T(8,128)S(1)}, u32[]{:S(2)}, u32[]{:S(2)}) collective-permute-start(f32[64,256]{0,1:T(8,128)S(1)} %bitcast.455), channel_id=1, source_target_pairs={{0,64},{1,65},{2,66},{3,67},{4,68},{5,69},{6,70},{7,71},{8,72},{9,... | collective-permute-start | bytes 196616 | tf_op jit(solution)/shard_map/ppermute | solution.py:32
  546.6 15.7 %collective-permute-start.41 = (f32[64,256]{0,1:T(8,128)S(1)}, f32[64,256]{0,1:T(8,128)S(1)}, u32[]{:S(2)}, u32[]{:S(2)}) collective-permute-start(f32[64,256]{0,1:T(8,128)S(1)} %bitcast.454), channel_id=1, source_target_pairs={{0,128},{1,129},{2,130},{3,131},{4,132},{5,133},{6,134},{7,135},{8... | collective-permute-start | bytes 196616 | tf_op jit(solution)/shard_map/ppermute | solution.py:32
  548.5 15.9 %collective-permute-start.42 = (f32[64,256]{0,1:T(8,128)S(1)}, f32[64,256]{0,1:T(8,128)S(1)}, u32[]{:S(2)}, u32[]{:S(2)}) collective-permute-start(f32[64,256]{0,1:T(8,128)S(1)} %bitcast.453), channel_id=1, source_target_pairs={{0,192},{1,193},{2,194},{3,195},{4,196},{5,197},{6,198},{7,199},{8... | collective-permute-start | bytes 196616 | tf_op jit(solution)/shard_map/ppermute | solution.py:32
  564.6 14.0 %collective-permute-start.43 = (f32[64,256]{1,0:T(8,128)S(1)}, f32[64,256]{1,0:T(8,128)S(1)}, u32[]{:S(2)}, u32[]{:S(2)}) collective-permute-start(f32[64,256]{1,0:T(8,128)S(1)} %bitcast.456), channel_id=1, source_target_pairs={{0,0},{1,17},{2,34},{3,51},{4,68},{5,85},{6,102},{7,119},{8,136},{... | collective-permute-start | bytes 196616 | tf_op jit(solution)/shard_map/ppermute | solution.py:32
  567.8 37.4 %collective-permute-start.47 = (f32[64,256]{0,1:T(8,128)S(1)}, f32[64,256]{0,1:T(8,128)S(1)}, u32[]{:S(2)}, u32[]{:S(2)}) collective-permute-start(f32[64,256]{0,1:T(8,128)S(1)} %fusion.108), channel_id=1, source_target_pairs={{0,4},{1,21},{2,38},{3,55},{4,64},{5,81},{6,98},{7,115},{8,140},{9... | collective-permute-start | bytes 196616 | tf_op jit(solution)/shard_map/ppermute | solution.py:32
  574.5 30.8 %collective-permute-start.48 = (f32[64,256]{0,1:T(8,128)S(1)}, f32[64,256]{0,1:T(8,128)S(1)}, u32[]{:S(2)}, u32[]{:S(2)}) collective-permute-start(f32[64,256]{0,1:T(8,128)S(1)} %fusion.108), channel_id=1, source_target_pairs={{16,4},{17,21},{18,38},{19,55},{20,64},{21,81},{22,98},{23,115},{2... | collective-permute-start | bytes 196616 | tf_op jit(solution)/shard_map/ppermute | solution.py:32
  575.8 29.5 %collective-permute-start.49 = (f32[64,256]{0,1:T(8,128)S(1)}, f32[64,256]{0,1:T(8,128)S(1)}, u32[]{:S(2)}, u32[]{:S(2)}) collective-permute-start(f32[64,256]{0,1:T(8,128)S(1)} %fusion.108), channel_id=1, source_target_pairs={{32,4},{33,21},{34,38},{35,55},{36,64},{37,81},{38,98},{39,115},{4... | collective-permute-start | bytes 196616 | tf_op jit(solution)/shard_map/ppermute | solution.py:32
  577.1 28.2 %collective-permute-start.50 = (f32[64,256]{0,1:T(8,128)S(1)}, f32[64,256]{0,1:T(8,128)S(1)}, u32[]{:S(2)}, u32[]{:S(2)}) collective-permute-start(f32[64,256]{0,1:T(8,128)S(1)} %fusion.108), channel_id=1, source_target_pairs={{48,4},{49,21},{50,38},{51,55},{52,64},{53,81},{54,98},{55,115},{5... | collective-permute-start | bytes 196616 | tf_op jit(solution)/shard_map/ppermute | solution.py:32
  593.1 12.0 %collective-permute-start.46 = (f32[64,256]{1,0:T(8,128)S(1)}, f32[64,256]{1,0:T(8,128)S(1)}, u32[]{:S(2)}, u32[]{:S(2)}) collective-permute-start(f32[64,256]{1,0:T(8,128)S(1)} %bitcast.457), channel_id=1, source_target_pairs={{0,32},{1,49},{2,66},{3,83},{4,100},{5,117},{6,6},{7,23},{8,168},{... | collective-permute-start | bytes 196616 | tf_op jit(solution)/shard_map/ppermute | solution.py:32
  606.9 37.6 %all-to-all-start = ((f32[16,32,256]{2,1,0:T(8,128)}), f32[16,32,256]{2,1,0:T(8,128)S(1)}, u32[]{:S(2)}, u32[]{:S(2)}) async-start(f32[16,32,256]{2,1,0:T(8,128)} %bitcast.147), calls=%async_computation | async-start | bytes 1048576 | tf_op jit(solution)/shard_map/all_to_all | solution.py:247
  (47 other events, 399.9 us)
